TPU v7x, 256 devices: a whole 4x4x8 slice. The times are simulated.
256 devices in a mesh: ex: 16 (over x_hi, y, core), tp: 16 (over z, x_lo).
Axes of the slice: x: 4 (x_hi: 2, x_lo: 2; x = x_hi * 2 + x_lo), y: 4, z: 8, core: 2. Of those that a mesh axis runs over, the one named last changes fastest.
Arguments:
- act: bfloat16 [4096, 7168], P('ex', 'tp'), may hold values from -6 to 6
- grad_out: bfloat16 [4096, 7168], P('ex'), may hold values from -6 to 6
- q_cols: float32 [128, 8], replicated, may hold values from -0.09375 to 0.09375
- example_order: int32 [128], replicated, may hold values from 0 to 127, each once
- segment: int32 [4096], P('ex'), may hold values from 0 to 127, never falling along the last dimension, each value on 1 to 48 neighbouring positions
Outputs:
- sketch: bfloat16 [7168, 8, 7168], P('tp', None, 'ex')
Inputs may be any that keep to these rules, and one draw needn't show every extreme that they name: example_order holds each number of 0 to 127 once. segment never falls along the tokens; each example has 1 to 48 tokens.
All inputs are finite; a program needn't handle non-finite values.
Results may differ from a plain program's by a relative error of at most 0.0049.
Values may be sent and summed in bfloat16 or wider, within the bound.
A program may use at most 128 MiB of HBM per device.

v0:
```python
import jax
import jax.numpy as jnp
from jax import lax
from jax.sharding import PartitionSpec as P


def local(act, grad_out, q_cols, example_order, segment):
    n_ex = lax.axis_size("ex")
    examples = q_cols.shape[0]
    columns_k = q_cols.shape[1]
    width_in = act.shape[1]
    width_out = grad_out.shape[1] // n_ex
    labels = jnp.arange(examples, dtype=jnp.int32)
    picks = (example_order[:, None] == labels[None, :]).astype(jnp.float32)
    q_ordered = jnp.dot(picks, q_cols, precision=lax.Precision.HIGHEST)
    grad_cols = lax.all_to_all(grad_out, "ex", split_axis=1, concat_axis=0, tiled=True)
    all_act, all_seg = (
        lax.all_gather(act, "ex", axis=0, tiled=True),
        lax.all_gather(segment, "ex", axis=0, tiled=True),
    )
    count = all_act.shape[0]
    onehot = (all_seg[:, None] == labels[None, :]).astype(jnp.float32)
    weight = jnp.dot(onehot, q_ordered, precision=lax.Precision.HIGHEST)
    scaled = (weight[:, :, None] * grad_cols[:, None, :].astype(jnp.float32)).astype(jnp.bfloat16)
    scaled = scaled.reshape(count, columns_k * width_out)
    total = lax.dot_general(
        all_act, scaled, (((0,), (0,)), ((), ())), preferred_element_type=jnp.float32
    )
    return total.reshape(width_in, columns_k, width_out).astype(jnp.bfloat16)


def solution(mesh):
    in_specs = (P("ex", "tp"), P("ex", None), P(), P(), P("ex"))
    out_specs = P("tp", None, "ex")
    return jax.shard_map(local, mesh=mesh, in_specs=in_specs, out_specs=out_specs, check_vma=False)
```

profile of v0, /device:TPU:1, one launch (start us, length us, event | category | flops | bytes accessed | tf_op | source)
XLA Modules:
  0.0 142.6 jit_solution(2439030485605400777)
XLA Ops:
  6.5 0.0 copy-start
  6.5 0.0 copy-start.1
  6.5 0.0 copy-start.2
  6.5 5.9 %copy.9 = bf16[256,7168]{0,1:T(8,128)(2,1)} copy(bf16[256,7168]{1,0:T(8,128)(2,1)} %param.6) | data formatting | bytes 7340032 | tf_op args[1]
  12.5 8.4 %all-to-all-start = ((bf16[256,16,448]{0,2,1:T(8,128)(2,1)}), bf16[256,16,448]{0,2,1:T(8,128)(2,1)}, u32[]{:S(2)}, u32[]{:S(2)}) async-start(bf16[256,16,448]{0,2,1:T(8,128)(2,1)} %bitcast.16), calls=%async_computation | async-start | bytes 7340032 | tf_op jit(solution)/shard_map/all_to_all | solution.py:16
  20.9 0.0 all-gather.3.cloned.1.call-start
  21.0 0.7 all-gather.3.cloned.1.call-update
  21.7 0.0 copy-done.1
  21.7 64.6 %all-gather = s32[16,1,256]{2,1,0:T(1,128)S(1)} all-gather(s32[1,1,256]{2,1,0:T(1,128)S(1)} %bitcast.18), channel_id=1, replica_groups=mesh['ex'=16,'tp'=16] {'ex'}, dimensions={0}, use_global_device_ids=true | all-gather | bytes 17408 | tf_op jit(solution)/shard_map/all_gather | solution.py:19
  86.2 0.0 copy-done
  86.2 0.0 copy-done.2
  86.2 0.2 fusion.3
  86.4 1.9 %fusion.1 = f32[4096,8]{0,1:T(8,128)S(1)} fusion(f32[128,8]{0,1:T(8,128)S(1)} %fusion.3, s32[4096]{0:T(1024)S(1)} %bitcast.17), kind=kOutput, calls=%fused_computation.5 | convolution fusion | flops 50855936 | bytes 151552 | tf_op jit(solution)/shard_map/dot_general | solution.py:23
  88.3 0.0 all-to-all-done
  88.3 3.0 %convert_bitcast_fusion = f32[16,56,8,256]{3,2,1,0:T(8,128)S(1)} fusion(bf16[256,16,448]{0,2,1:T(8,128)(2,1)} %all-to-all-done), kind=kLoop, calls=%fused_computation.1 | loop fusion | flops 1835008 | bytes 11010048
  91.3 0.9 copy.11
  92.2 10.1 %multiply_convert_fusion = bf16[4096,8,448]{0,2,1:T(8,128)(2,1)} fusion(f32[4096,448]{0,1:T(8,128)S(1)} %bitcast.15, f32[4096,8]{0,1:T(8,128)S(1)} %fusion.1), kind=kLoop, calls=%fused_computation | loop fusion | flops 29360128 | bytes 36831232 | tf_op jit(solution)/shard_map/convert_element_type | solution.py:24
  102.3 8.3 %all-gather.3.cloned.1.call-done = bf16[4096,448]{0,1:T(8,128)(2,1)} async-done(((bf16[256,448]{0,1:T(8,128)(2,1)}), bf16[4096,448]{0,1:T(8,128)(2,1)}) %all-gather.3.cloned.1.call-update) | async-done | bytes 3670032 | tf_op jit(solution)/shard_map/all_gather | solution.py:18
  110.6 19.9 %fusion = bf16[448,3584]{1,0:T(8,128)(2,1)S(1)} fusion(bf16[4096,3584]{0,1:T(8,128)(2,1)} %bitcast.14, bf16[4096,448]{0,1:T(8,128)(2,1)} %all-gather.3.cloned.1.call-done), kind=kOutput, calls=%fused_computation.3 | convolution fusion | flops 13154942976 | bytes 36241408 | tf_op jit(solution)/shard_map/dot_general | solution.py:26
  130.5 5.3 %convert_element_type.39 = bf16[448,8,448]{2,1,0:T(8,128)(2,1)} reshape(bf16[448,3584]{1,0:T(8,128)(2,1)S(1)} %fusion) | data formatting | bytes 6422528 | tf_op jit(solution)/shard_map/convert_element_type | solution.py:29
Async XLA Ops:
  6.5 79.7 %copy-start = (f32[128,8]{0,1:T(8,128)S(1)}, f32[128,8]{0,1:T(8,128)}, u32[]{:S(2)}) copy-start(f32[128,8]{0,1:T(8,128)} %param.7) | copy-start | bytes 12292
  6.5 15.1 %copy-start.1 = (s32[256]{0:T(256)S(1)}, s32[256]{0:T(256)}, u32[]{:S(2)}) copy-start(s32[256]{0:T(256)} %param.9) | copy-start | bytes 3076
  6.5 79.7 %copy-start.2 = (s32[128]{0:T(128)S(1)}, s32[128]{0:T(128)}, u32[]{:S(2)}) copy-start(s32[128]{0:T(128)} %param.8) | copy-start | bytes 1540
  12.5 75.9 %all-to-all-start = ((bf16[256,16,448]{0,2,1:T(8,128)(2,1)}), bf16[256,16,448]{0,2,1:T(8,128)(2,1)}, u32[]{:S(2)}, u32[]{:S(2)}) async-start(bf16[256,16,448]{0,2,1:T(8,128)(2,1)} %bitcast.16), calls=%async_computation | async-start | bytes 7340032 | tf_op jit(solution)/shard_map/all_to_all | solution.py:16
  20.9 89.7 %all-gather.3.cloned.1.call-start = ((), (), s32[]{:S(2)}) async-start(), calls=%async_computation.1 | async-start | bytes 3899392 | tf_op jit(solution)/shard_map/all_gather | solution.py:18
Sparse Core Ops, SparseCore 0:
  24.3 86.2 all-gather.2
where the time goes:
time: 143 us
  blocking collectives  64.6 us (45%)
  matrix products  22 us (15%)
  between operations  13.4 us (9%)
  other arithmetic  13 us (9%)
  local copies, waits for them, and re-layouts  12.1 us (8%)
  waiting for transfers between devices  9 us (6%)
  starting transfers between devices  8.48 us (6%)
    all_gather x1, blocking collectives, local(): lax.all_gather(segment, 'ex', axis=0, tiled=True)  64.6 us
    dot_general x1, matrix products, local(): lax.dot_general(all_act, scaled, (((0,), (0,)), ((), ())), preferred_elem...  19.9 us
    convert_element_type x1, other arithmetic, local(): (weight[:, :, None] * grad_cols[:, None, :].astype(jnp.float32)).astype(j...  10.1 us
    all_to_all x1, starting transfers between devices, local(): lax.all_to_all(grad_out, 'ex', split_axis=1, concat_axis=0, tiled=True)  8.45 us
    all_gather x1, waiting for transfers between devices, local(): lax.all_gather(act, 'ex', axis=0, tiled=True)  8.32 us
    unnamed x7, local copies, waits for them, and re-layouts  5.94 us
    convert_element_type x1, local copies, waits for them, and re-layouts, local(): return total.reshape(width_in, columns_k, width_out).astype(jnp.bfloat16)  5.31 us
    unnamed x1, other arithmetic  2.95 us
  transfers between devices with their start and end apart: 2, of which 1 were waited for; matrix products, arithmetic and copies ran while one was open for 11% of the time, Pallas kernels for 0%

commit v1 on v0

v1 whole, which is shorter than its diff:
```python
import jax
import jax.numpy as jnp
from jax import lax
from jax.experimental import pallas as pl
from jax.experimental.pallas import tpu as pltpu
from jax.sharding import PartitionSpec as P

MESH = pl.DeviceIdType.MESH
BF16, F32 = jnp.bfloat16, jnp.float32
NX, NY, NZ = 2, 4, 8
GROUPS = NX * NY
TOK = 256
WIN = 448
SLAB = 896
HALF = 512
MSG = 480
SHARE = TOK // 4
K = 8
BLOCK = 64


def ring(q):
    return q + q // 2 - 2 * (q // 3)


def kernel(
    act, grad, q_cols, order, segment, out,
    a_buf, g_buf, h_buf, rhs, acc, stage,
    local_sem, out_sem,
    a_send, a_recv, as_send, as_recv, d_send, d_recv, z_send, z_recv, h_send, h_recv,
):
    e, t = lax.axis_index("ex"), lax.axis_index("tp")
    xh, y, c = e // 8, (e // 2) % 4, e % 2
    z, xl = t // 2, t % 2
    share = z % 4

    def dev(dx=0, dy=0, dz=0, dc=0):
        return (
            ((xh + dx) % NX) * 8 + ((y + dy) % NY) * 2 + (c + dc) % 2,
            ((z + dz) % NZ) * 2 + xl,
        )

    def remote(src, dst, send, recv, to):
        return pltpu.make_async_remote_copy(
            src_ref=src, dst_ref=dst, send_sem=send, recv_sem=recv,
            device_id=to, device_id_type=MESH,
        )

    barrier = pltpu.get_barrier_semaphore()
    peers = [dev(dx, dy) for dy in range(NY) for dx in range(NX) if (dx, dy) != (0, 0)]
    peers += [dev(dz=1), dev(dz=-1), dev(dc=1)]
    for peer in peers:
        pl.semaphore_signal(barrier, inc=1, device_id=peer, device_id_type=MESH)

    own = pl.ds(0, TOK)
    other = pl.ds(TOK, TOK)
    act_in = pltpu.make_async_copy(act, a_buf.at[0, pl.ds(0, WIN), own], local_sem.at[0])
    act_in.start()
    slab = pl.multiple_of(SLAB * (4 * xh + y), 128)
    grad_in = pltpu.make_async_copy(grad.at[:, pl.ds(slab, SLAB)], g_buf.at[0], local_sem.at[1])
    grad_in.start()

    labels = lax.broadcasted_iota(jnp.int32, (128, TOK), 0)
    in_example = (jnp.broadcast_to(segment[...], (128, TOK)) == labels).astype(F32).astype(BF16)
    order_rows = jnp.broadcast_to(order[...].astype(F32), (16, 128)).astype(BF16)
    rows = jnp.dot(order_rows, in_example, preferred_element_type=F32)
    picked = jnp.broadcast_to(rows[0:1, :], (128, TOK)) == labels.astype(F32)
    q = q_cols[...]
    q1 = q.astype(BF16).astype(F32)
    q2 = (q - q1).astype(BF16).astype(F32)
    q3 = q - q1 - q2
    parts = jnp.concatenate([q1, q2, q3, jnp.zeros_like(q)], axis=0).astype(BF16)
    weights = jnp.dot(parts, picked.astype(F32).astype(BF16), preferred_element_type=F32)
    a_buf[0, pl.ds(WIN, MSG - WIN), own] = weights.astype(BF16)
    act_in.wait()

    pl.semaphore_wait(barrier, len(peers))

    def direct(r):
        dx, dy = r % 2, ring(r // 2)
        to_x, to_y = (xh + dx) % NX, (y - dy + NY) % NY
        lanes = pl.ds(pl.multiple_of(SLAB * (4 * to_x + to_y), 128), SLAB)
        mine = pl.ds(pl.multiple_of(SHARE * share, SHARE), SHARE)
        return remote(
            grad.at[mine, lanes], g_buf.at[r, mine, :], d_send.at[r], d_recv.at[r],
            (to_x * 8 + to_y * 2 + c, t),
        )

    def along_z(r, hop, way):
        if hop == 0:
            at = pl.ds(pl.multiple_of(SHARE * share, SHARE), SHARE)
        else:
            of = (share + (3 if way == 0 else 1)) % 4
            at = pl.ds(pl.multiple_of(SHARE * of + (SHARE // 2) * way, SHARE // 2), SHARE // 2)
        part = g_buf.at[r, at, :]
        i = hop * 2 + way
        return remote(part, part, z_send.at[r, i], z_recv.at[r, i], dev(dz=1 if way == 0 else -1))

    def to_sibling(r):
        lanes = pl.ds(pl.multiple_of(384 * (1 - c), 128), HALF)
        return remote(g_buf.at[r, :, lanes], h_buf.at[r], h_send.at[r], h_recv.at[r], dev(dc=1))

    def act_whole(i):
        src, dst, to = [
            (0, 1, dev(dx=1)),
            (0, 4, dev(dy=1)), (0, 2, dev(dy=-1)),
            (1, 5, dev(dy=1)), (1, 3, dev(dy=-1)),
        ][i]
        return remote(a_buf.at[src, :, own], a_buf.at[dst, :, own], a_send.at[i], a_recv.at[i], to)

    def act_half(i):
        src, dst, to, at = [
            (4, 6, dev(dy=1), 0), (2, 6, dev(dy=-1), MSG // 2),
            (5, 7, dev(dy=1), 0), (3, 7, dev(dy=-1), MSG // 2),
        ][i]
        at = pl.ds(at, MSG // 2)
        return remote(
            a_buf.at[src, at, own], a_buf.at[dst, at, own], a_send.at[5 + i], a_recv.at[5 + i], to
        )

    def act_sibling(r):
        return remote(
            a_buf.at[r, :, own], a_buf.at[r, :, other], as_send.at[r], as_recv.at[r], dev(dc=1)
        )

    act_whole(0).start()
    lax.fori_loop(1, GROUPS, lambda r, _: (direct(r).start(), 0)[1], 0)
    act_whole(1).start()
    act_whole(2).start()
    act_sibling(0).start()
    grad_in.wait()
    to_sibling(0).start()

    rhs[...] = jnp.zeros_like(rhs)
    acc[...] = jnp.zeros_like(acc)

    def load_rhs(r):
        @pl.when(c == 0)
        def _():
            rhs[0:TOK, :] = g_buf[r, :, 0:HALF]
            rhs[TOK:, :] = h_buf[r]

        @pl.when(c == 1)
        def _():
            rhs[0:TOK, 0:WIN] = g_buf[r, :, SLAB - WIN:SLAB]
            rhs[TOK:, 0:WIN] = h_buf[r, :, HALF - WIN:HALF]

    def product(r, i):
        w = a_buf[r, WIN:WIN + 32, :].astype(F32)
        w = w[0:8] + w[8:16] + w[16:24]
        part = a_buf[r, pl.ds(i * BLOCK, BLOCK), :].astype(F32)
        left = (part[:, None, :] * w[None, :, :]).reshape(BLOCK * K, 2 * TOK).astype(BF16)
        return jnp.dot(left, rhs[...], preferred_element_type=F32)

    def compute(r):
        load_rhs(r)
        for i in range(WIN // BLOCK):
            acc[pl.ds(i * BLOCK * K, BLOCK * K), :] += product(r, i)

    def out_copy(i):
        at = pl.ds(i * BLOCK, BLOCK)
        return pltpu.make_async_copy(stage.at[at], out.at[at], out_sem.at[i])

    def compute_last(r):
        load_rhs(r)
        for i in range(WIN // BLOCK):
            total = acc[pl.ds(i * BLOCK * K, BLOCK * K), :] + product(r, i)
            stage[pl.ds(i * BLOCK, BLOCK)] = total[:, 0:WIN].reshape(BLOCK, K, WIN).astype(BF16)
            out_copy(i).start()

    def tick(n, _):
        @pl.when(n <= 7)
        def _():
            direct(n).wait_recv()
            along_z(n, 0, 0).start()
            along_z(n, 0, 1).start()

        @pl.when(n == 1)
        def _():
            act_whole(0).wait_recv()
            act_whole(3).start()
            act_whole(4).start()
            act_sibling(1).start()

        @pl.when(n == 2)
        def _():
            act_whole(1).wait_recv()
            act_half(0).start()
            act_sibling(4).start()
            act_whole(2).wait_recv()
            act_half(1).start()
            act_sibling(2).start()

        @pl.when(n == 4)
        def _():
            act_whole(3).wait_recv()
            act_half(2).start()
            act_sibling(5).start()
            act_whole(4).wait_recv()
            act_half(3).start()
            act_sibling(3).start()

        @pl.when(n == 7)
        def _():
            act_half(0).wait_recv()
            act_half(1).wait_recv()
            act_sibling(6).start()

        @pl.when(n == 8)
        def _():
            act_half(2).wait_recv()
            act_half(3).wait_recv()
            act_sibling(7).start()

        @pl.when((n >= 2) & (n <= 8))
        def _():
            r = n - 1
            along_z(r, 0, 0).wait_recv()
            along_z(r, 1, 0).start()
            along_z(r, 0, 1).wait_recv()
            along_z(r, 1, 1).start()

        @pl.when((n >= 3) & (n <= 9))
        def _():
            r = n - 2
            along_z(r, 1, 0).wait_recv()
            along_z(r, 1, 1).wait_recv()
            to_sibling(r).start()

        @pl.when((n == 1) | (n >= 4))
        def _():
            r = jnp.where(n == 1, 0, n - 3)
            act_sibling(r).wait_recv()
            to_sibling(r).wait_recv()
            compute(r)

        return 0

    lax.fori_loop(1, GROUPS + 2, tick, 0)
    act_sibling(GROUPS - 1).wait_recv()
    to_sibling(GROUPS - 1).wait_recv()
    compute_last(GROUPS - 1)

    for i in range(5):
        act_whole(i).wait_send()
    for i in range(4):
        act_half(i).wait_send()

    def drain(r, _):
        act_sibling(r).wait_send()
        to_sibling(r).wait_send()

        @pl.when(r > 0)
        def _():
            direct(r).wait_send()
            for hop in range(2):
                for way in range(2):
                    along_z(r, hop, way).wait_send()

        return 0

    lax.fori_loop(0, GROUPS, drain, 0)
    for i in range(WIN // BLOCK):
        out_copy(i).wait()


def local(act, grad_out, q_cols, example_order, segment):
    dma = pltpu.SemaphoreType.DMA
    return pl.pallas_call(
        kernel,
        out_shape=jax.ShapeDtypeStruct((WIN, K, WIN), BF16),
        in_specs=[pl.BlockSpec(memory_space=pl.ANY)] * 2 + [pl.BlockSpec(memory_space=pltpu.VMEM)] * 3,
        out_specs=pl.BlockSpec(memory_space=pl.ANY),
        scratch_shapes=[
            pltpu.VMEM((GROUPS, MSG, 2 * TOK), BF16),
            pltpu.VMEM((GROUPS, TOK, SLAB), BF16),
            pltpu.VMEM((GROUPS, TOK, HALF), BF16),
            pltpu.VMEM((2 * TOK, HALF), BF16),
            pltpu.VMEM((WIN * K, HALF), F32),
            pltpu.VMEM((WIN, K, WIN), BF16),
            dma((2,)), dma((WIN // BLOCK,)),
            dma((9,)), dma((9,)), dma((GROUPS,)), dma((GROUPS,)),
            dma((GROUPS,)), dma((GROUPS,)), dma((GROUPS, 4)), dma((GROUPS, 4)),
            dma((GROUPS,)), dma((GROUPS,)),
        ],
        compiler_params=pltpu.CompilerParams(
            collective_id=1, has_side_effects=True, vmem_limit_bytes=48 * 1024 * 1024
        ),
    )(act.T, grad_out, q_cols.T, example_order[None, :], segment[None, :])


def solution(mesh):
    in_specs = (P("ex", "tp"), P("ex", None), P(), P(), P("ex"))
    out_specs = P("tp", None, "ex")
    return jax.shard_map(local, mesh=mesh, in_specs=in_specs, out_specs=out_specs, check_vma=False)
```

time: 143 us -> 64.4 us (0.45)
  blocking collectives: 64.6 us -> 0 us
  Pallas kernels: 0 us -> 59.4 us
  matrix products: 22 us -> 0 us
  between operations: 13.4 us -> 0.01 us
  other arithmetic: 13 us -> 0 us
  waiting for transfers between devices: 9 us -> 0 us
  starting transfers between devices: 8.48 us -> 0 us
  local copies, waits for them, and re-layouts: 12.1 us -> 4.8 us
    all_gather x1 -> x0, blocking collectives: 64.6 us -> none  [local(): lax.all_gather(segment, 'ex', axis=0, tiled=True)]
    pallas_call x0 -> x1, Pallas kernels: none -> 59.4 us  [local(): pl.pallas_call(kernel, out_shape=jax.ShapeDtypeStruct((WIN, K, WIN), BF16...]
    dot_general x3 -> x0, matrix products: 22 us -> none  [the longest x1 19.9 us: local(): lax.dot_general(all_act, scaled, (((0,), (0,)), ((), ())), preferred_elem...]
    convert_element_type x1 -> x0, other arithmetic: 10.1 us -> none  [local(): (weight[:, :, None] * grad_cols[:, None, :].astype(jnp.float32)).astype(j...]
    all_to_all x1 -> x0, starting transfers between devices: 8.45 us -> none  [local(): lax.all_to_all(grad_out, 'ex', split_axis=1, concat_axis=0, tiled=True)]
    all_gather x1 -> x0, waiting for transfers between devices: 8.32 us -> none  [local(): lax.all_gather(act, 'ex', axis=0, tiled=True)]
    convert_element_type x2 -> x0, local copies, waits for them, and re-layouts: 6.18 us -> none  [the longest x1 5.31 us: local(): return total.reshape(width_in, columns_k, width_out).astype(jnp.bfloat16)]
    unnamed x1 -> x0, other arithmetic: 2.95 us -> none
  transfers between devices with their start and end apart: 2 -> 0, of which waited for: 1 -> 0; matrix products, arithmetic and copies ran while one was open for 11% -> 0% of each run, Pallas kernels for 0% -> 0%
where the time goes in v1:
time: 64.4 us; the launch traced here: 64.2 us
  Pallas kernels  59.4 us (92%)
  local copies, waits for them, and re-layouts  4.8 us (7%)
    pallas_call x1, Pallas kernels, local(): pl.pallas_call(kernel, out_shape=jax.ShapeDtypeStruct((WIN, K, WIN), BF16...  59.4 us
    unnamed x9, local copies, waits for them, and re-layouts  4.8 us

profile of v1, /device:TPU:1, one launch (start us, length us, event | category | flops | bytes accessed | tf_op | source)
XLA Modules:
  0.0 64.2 jit_solution(13762763892028980897)
XLA Ops:
  0.0 0.0 copy-start
  0.0 0.9 %copy-done = bf16[256,448]{0,1:T(8,128)(2,1)S(1)} copy-done((bf16[256,448]{0,1:T(8,128)(2,1)S(1)}, bf16[256,448]{0,1:T(8,128)(2,1)}, u32[]{:S(2)}) %copy-start) | copy-done | bytes 229400
  0.9 0.0 copy-start.1
  0.9 0.7 %copy-done.1 = f32[128,8]{0,1:T(8,128)S(1)} copy-done((f32[128,8]{0,1:T(8,128)S(1)}, f32[128,8]{0,1:T(8,128)}, u32[]{:S(2)}) %copy-start.1) | copy-done | bytes 4120
  1.6 0.0 copy-start.2
  1.6 0.7 %copy-done.2 = s32[256]{0:T(256)S(1)} copy-done((s32[256]{0:T(256)S(1)}, s32[256]{0:T(256)}, u32[]{:S(2)}) %copy-start.2) | copy-done | bytes 1048
  2.3 0.0 copy-start.3
  2.3 0.7 %copy-done.3 = s32[128]{0:T(128)S(1)} copy-done((s32[128]{0:T(128)S(1)}, s32[128]{0:T(128)}, u32[]{:S(2)}) %copy-start.3) | copy-done | bytes 536
  3.0 59.4 %shard_map.55 = bf16[448,8,448]{2,1,0:T(8,128)(2,1)S(1)} custom-call(bf16[448,256]{1,0:T(8,128)(2,1)S(1)} %bitcast.4, bf16[256,7168]{1,0:T(8,128)(2,1)} %grad.1, f32[8,128]{1,0:T(8,128)S(1)} %bitcast.5, s32[1,128]{1,0:T(1,128)S(1)} %bitcast.7, s32[1,256]{1,0:T(1,128)S(1)} %bitcast.6), custom_call_target="tpu_custom_call" | custom-call | tf_op jit(solution)/shard_map/pallas_call | solution.py:269
  62.3 1.8 %copy.7 = bf16[448,8,448]{2,1,0:T(8,128)(2,1)} copy(bf16[448,8,448]{2,1,0:T(8,128)(2,1)S(1)} %shard_map.55) | data formatting | bytes 6422528
Async XLA Ops:
  0.0 0.9 %copy-start = (bf16[256,448]{0,1:T(8,128)(2,1)S(1)}, bf16[256,448]{0,1:T(8,128)(2,1)}, u32[]{:S(2)}) copy-start(bf16[256,448]{0,1:T(8,128)(2,1)} %param.5) | copy-start | bytes 688132
  0.9 0.7 %copy-start.1 = (f32[128,8]{0,1:T(8,128)S(1)}, f32[128,8]{0,1:T(8,128)}, u32[]{:S(2)}) copy-start(f32[128,8]{0,1:T(8,128)} %param.7) | copy-start | bytes 12292
  1.6 0.7 %copy-start.2 = (s32[256]{0:T(256)S(1)}, s32[256]{0:T(256)}, u32[]{:S(2)}) copy-start(s32[256]{0:T(256)} %param.9) | copy-start | bytes 3076
  2.3 0.7 %copy-start.3 = (s32[128]{0:T(128)S(1)}, s32[128]{0:T(128)}, u32[]{:S(2)}) copy-start(s32[128]{0:T(128)} %param.8) | copy-start | bytes 1540

commit v2 on v0

v2 whole, which is shorter than its diff:
```python
import jax
import jax.numpy as jnp
from jax import lax
from jax.experimental import pallas as pl
from jax.experimental.pallas import tpu as pltpu
from jax.sharding import PartitionSpec as P

MESH = pl.DeviceIdType.MESH
BF16, F32 = jnp.bfloat16, jnp.float32
NX, NY, NZ = 2, 4, 8
TOK = 256
WIN = 448
SLAB = 896
HALF = 512
MSG = 480
K = 8
BLOCK = 112
WIDE = 224
SOURCES = ((0, 0), (0, 1), (0, 3), (1, 0), (1, 1), (1, 3), (0, 2), (1, 2))
GROUPS = len(SOURCES)
WHOLE = (3,)
SPLIT = (2, 4, 7)
GO, GET = True, False
FIRST = (
    (GO, 'act_core', 0),
    (GO, 'columns', 0),
    (GO, 'direct', 4),
    (GO, 'direct', 2),
    (GO, 'act', 0),
    (GO, 'direct', 7),
    (GO, 'direct', 5),
    (GO, 'act', 1),
    (GO, 'direct', 1),
    (GO, 'act', 2),
)
STEPS = (
    ((), 0, 0),
    ((
        (GET, 'act_core', 0),
        (GET, 'columns', 0),
    ), 0, 1),
    ((
        (GET, 'direct', 2),
        (GO, 'z_first', 2, 1),
        (GO, 'z_first', 2, 0),
        (GET, 'direct', 4),
        (GO, 'z_first', 4, 0),
        (GO, 'z_first', 4, 1),
        (GO, 'direct', 3),
        (GO, 'direct', 6),
        (GET, 'z_first', 2, 1),
        (GET, 'z_first', 2, 0),
        (GO, 'z_second', 2, 0),
        (GO, 'z_second', 2, 1),
        (GET, 'direct', 1),
        (GO, 'z_first', 1, 0),
        (GO, 'z_first', 1, 1),
        (GET, 'z_first', 4, 0),
        (GET, 'z_first', 4, 1),
        (GO, 'z_second', 4, 1),
        (GO, 'z_second', 4, 0),
        (GET, 'z_second', 2, 0),
        (GET, 'z_second', 2, 1),
        (GO, 'x_lo', 2),
        (GET, 'act', 0),
        (GO, 'act_core', 3),
        (GO, 'act', 4),
        (GET, 'direct', 7),
        (GO, 'act', 3),
        (GO, 'z_first', 7, 0),
        (GO, 'z_first', 7, 1),
        (GET, 'act_core', 3),
        (GET, 'z_first', 1, 0),
        (GET, 'z_first', 1, 1),
        (GO, 'z_second', 1, 1),
        (GO, 'z_second', 1, 0),
        (GET, 'z_second', 4, 1),
        (GET, 'z_second', 4, 0),
        (GO, 'x_lo', 4),
        (GET, 'act', 1),
        (GO, 'act_core', 2),
        (GET, 'act', 2),
        (GO, 'act_core', 1),
        (GO, 'act_half', 0),
        (GO, 'act_half', 1),
        (GET, 'direct', 5),
        (GO, 'z_first', 5, 0),
        (GO, 'z_first', 5, 1),
        (GET, 'z_first', 7, 0),
        (GET, 'z_first', 7, 1),
        (GO, 'z_second', 7, 1),
        (GO, 'z_second', 7, 0),
        (GET, 'act_core', 2),
        (GET, 'act_core', 1),
        (GET, 'z_second', 1, 1),
        (GET, 'z_second', 1, 0),
        (GO, 'columns', 1),
    ), 1, 0),
    ((
        (GET, 'x_lo', 2),
        (GO, 'columns', 2),
        (GET, 'direct', 6),
        (GO, 'z_first', 6, 0),
        (GO, 'z_first', 6, 1),
    ), 2, 0),
    ((
        (GET, 'columns', 1),
        (GET, 'z_first', 5, 0),
        (GET, 'z_first', 5, 1),
        (GO, 'z_second', 5, 0),
        (GO, 'z_second', 5, 1),
    ), 1, 1),
    ((
        (GET, 'columns', 2),
        (GET, 'z_second', 7, 1),
        (GET, 'z_second', 7, 0),
        (GO, 'x_lo', 7),
    ), 2, 1),
    ((
        (GET, 'z_first', 6, 0),
        (GET, 'z_first', 6, 1),
        (GO, 'z_second', 6, 1),
        (GO, 'z_second', 6, 0),
        (GET, 'act', 4),
        (GO, 'act_core', 4),
        (GET, 'act', 3),
        (GO, 'act_core', 5),
        (GO, 'act_half', 3),
        (GO, 'act_half', 2),
        (GET, 'x_lo', 4),
        (GO, 'columns', 4),
    ), 4, 0),
    ((
        (GET, 'z_second', 5, 0),
        (GET, 'z_second', 5, 1),
        (GO, 'columns', 5),
    ), 5, 0),
    ((
        (GET, 'act_core', 4),
        (GET, 'act_core', 5),
        (GET, 'direct', 3),
        (GO, 'columns', 3),
        (GET, 'columns', 4),
    ), 4, 1),
    ((
        (GET, 'z_second', 6, 1),
        (GET, 'z_second', 6, 0),
        (GO, 'columns', 6),
        (GET, 'act_half', 0),
        (GET, 'act_half', 1),
        (GO, 'act_core', 6),
        (GET, 'columns', 5),
    ), 5, 1),
    ((
        (GET, 'columns', 3),
        (GET, 'x_lo', 7),
        (GO, 'columns', 7),
    ), 3, 2),
    ((
        (GET, 'act_half', 3),
        (GET, 'act_half', 2),
        (GO, 'act_core', 7),
        (GET, 'columns', 6),
        (GET, 'act_core', 6),
        (GET, 'columns', 7),
    ), 6, 2),
    ((
        (GET, 'act_core', 7),
    ), 7, 2),
)

def kernel(
    act, grad, q_cols, order, segment, out,
    a_buf, g_buf, h_buf, rhs, acc, q_buf, order_buf, segment_buf, local_sem,
    a_send, a_recv, as_send, as_recv, d_send, d_recv, z_send, z_recv, x_send, x_recv, h_send, h_recv,
):
    e, t = lax.axis_index("ex"), lax.axis_index("tp")
    xh, y, c = e // 8, (e // 2) % 4, e % 2
    z, xl = t // 2, t % 2
    share = z % 4

    def dev(dx=0, dy=0, dz=0, dc=0, dl=0):
        return (
            ((xh + dx) % NX) * 8 + ((y + dy + NY) % NY) * 2 + (c + dc) % 2,
            ((z + dz + NZ) % NZ) * 2 + (xl + dl) % 2,
        )

    def remote(src, dst, send, recv, to):
        return pltpu.make_async_remote_copy(
            src_ref=src, dst_ref=dst, send_sem=send, recv_sem=recv,
            device_id=to, device_id_type=MESH,
        )

    barrier = pltpu.get_barrier_semaphore()
    peers = [dev(dx, dy, dl=dx) for dx, dy in SOURCES[1:]]
    peers += [dev(dx=1), dev(dl=1), dev(dz=1), dev(dz=-1), dev(dc=1)]
    for peer in peers:
        pl.semaphore_signal(barrier, inc=1, device_id=peer, device_id_type=MESH)

    own = pl.ds(0, TOK)
    other = pl.ds(TOK, TOK)
    slab = pl.multiple_of(SLAB * (4 * xh + y), 128)
    loads = [
        pltpu.make_async_copy(src, dst, local_sem.at[i])
        for i, (src, dst) in enumerate([
            (order, order_buf), (segment, segment_buf), (q_cols, q_buf),
            (act, a_buf.at[0, pl.ds(0, WIN), own]),
            (grad.at[:, pl.ds(slab, SLAB)], g_buf.at[0]),
        ])
    ]
    for load in loads:
        load.start()
    rhs[...] = jnp.zeros_like(rhs)
    acc[...] = jnp.zeros_like(acc)
    for load in loads[:3]:
        load.wait()

    labels = lax.broadcasted_iota(jnp.int32, (128, TOK), 0)
    in_example = (jnp.broadcast_to(segment_buf[...], (128, TOK)) == labels).astype(F32).astype(BF16)
    order_rows = jnp.broadcast_to(order_buf[...].astype(F32), (16, 128)).astype(BF16)
    rows = jnp.dot(order_rows, in_example, preferred_element_type=F32)
    picked = jnp.broadcast_to(rows[0:1, :], (128, TOK)) == labels.astype(F32)
    q = q_buf[...]
    q1 = q.astype(BF16).astype(F32)
    q2 = (q - q1).astype(BF16).astype(F32)
    q3 = q - q1 - q2
    parts = jnp.concatenate([q1, q2, q3, jnp.zeros_like(q)], axis=0).astype(BF16)
    weights = jnp.dot(parts, picked.astype(F32).astype(BF16), preferred_element_type=F32)
    a_buf[0, pl.ds(WIN, MSG - WIN), own] = weights.astype(BF16)
    loads[3].wait()

    pl.semaphore_wait(barrier, len(peers))

    def quarter(r, q, side, half=None):
        if r in WHOLE:
            return pl.ds(0, TOK)
        rows = TOK // 8 if r in SPLIT else TOK // 4
        at = q * rows + (side * (TOK // 2) if r in SPLIT else 0)
        if half is not None:
            rows = rows // 2
            at = at + half * rows
        return pl.ds(pl.multiple_of(at, rows), rows)

    def direct(r):
        dx, dy = SOURCES[r]
        to_x, to_y = (xh + dx) % NX, (y - dy + NY) % NY
        lanes = pl.ds(pl.multiple_of(SLAB * (4 * to_x + to_y), 128), SLAB)
        rows = quarter(r, share, (xl + dx) % 2)
        return remote(
            grad.at[rows, lanes], g_buf.at[r, rows, :], d_send.at[r], d_recv.at[r], dev(dx, -dy, dl=dx)
        )

    def direct_in(r):
        part = g_buf.at[r, quarter(r, share, xl), :]
        return remote(part, part, d_send.at[r], d_recv.at[r], dev(dc=1))

    def along_z(r, hop, way):
        if hop == 0:
            at = quarter(r, share, xl)
        else:
            at = quarter(r, (share + (3 if way == 0 else 1)) % 4, xl, way)
        part = g_buf.at[r, at, :]
        i = hop * 2 + way
        return remote(part, part, z_send.at[r, i], z_recv.at[r, i], dev(dz=1 if way == 0 else -1))

    def to_x_lo(r):
        half = TOK // 2
        part = g_buf.at[r, pl.ds(pl.multiple_of(xl * half, half), half), :]
        return remote(part, part, x_send.at[r], x_recv.at[r], dev(dl=1))

    def to_sibling(r):
        lanes = pl.ds(pl.multiple_of(384 * (1 - c), 128), HALF)
        return remote(g_buf.at[r, :, lanes], h_buf.at[r], h_send.at[r], h_recv.at[r], dev(dc=1))

    def act_whole(i):
        src, dst, to = [
            (0, 3, dev(dx=1)),
            (0, 2, dev(dy=1)), (0, 1, dev(dy=-1)),
            (3, 5, dev(dy=1)), (3, 4, dev(dy=-1)),
        ][i]
        return remote(a_buf.at[src, :, own], a_buf.at[dst, :, own], a_send.at[i], a_recv.at[i], to)

    def act_half(i):
        src, dst, to, at = [
            (2, 6, dev(dy=1), 0), (1, 6, dev(dy=-1), MSG // 2),
            (5, 7, dev(dy=1), 0), (4, 7, dev(dy=-1), MSG // 2),
        ][i]
        at = pl.ds(at, MSG // 2)
        return remote(
            a_buf.at[src, at, own], a_buf.at[dst, at, own], a_send.at[5 + i], a_recv.at[5 + i], to
        )

    def act_sibling(r):
        return remote(
            a_buf.at[r, :, own], a_buf.at[r, :, other], as_send.at[r], as_recv.at[r], dev(dc=1)
        )

    transfers = {
        "direct": direct, "x_lo": to_x_lo, "columns": to_sibling,
        "z_first": lambda r, way: along_z(r, 0, way), "z_second": lambda r, way: along_z(r, 1, way),
        "act": act_whole, "act_half": act_half, "act_core": act_sibling,
    }

    def run(todo):
        for go, name, *which in todo:
            if go:
                transfers[name](*which).start()
            else:
                (direct_in if name == "direct" else transfers[name])(*which).wait_recv()

    run([item for item in FIRST if item[1:] != ("columns", 0)])
    loads[4].wait()
    to_sibling(0).start()

    def load_rhs(r, half):
        at = pl.ds(half * TOK, TOK)

        @pl.when(c == 0)
        def _():
            rhs[at, :] = g_buf[r, :, 0:HALF] if half == 0 else h_buf[r]

        @pl.when(c == 1)
        def _():
            rhs[at, 0:WIN] = g_buf[r, :, SLAB - WIN:SLAB] if half == 0 else h_buf[r, :, HALF - WIN:HALF]

    def product(r, row, size, at):
        w = a_buf[r, WIN:WIN + 32, at].astype(F32)
        w = w[0:8] + w[8:16] + w[16:24]
        part = a_buf[r, pl.ds(row, size), at].astype(F32)
        left = (part[:, None, :] * w[None, :, :]).astype(BF16).reshape(size * K, at.size)
        return jnp.dot(left, rhs[at, :], preferred_element_type=F32)

    def add(r, size, at):
        for row in range(0, WIN, size):
            acc[pl.ds(row * K, size * K), :] += product(r, row, size, at)

    def step(n, _):
        for i, (todo, _, _) in enumerate(STEPS[:-1]):
            if todo:
                pl.when(n == i)(lambda todo=todo: run(todo))
        r = sum(jnp.where(n == i, r, 0) for i, (_, r, _) in enumerate(STEPS[:-1]))
        mode = sum(jnp.where(n == i, mode, 0) for i, (_, _, mode) in enumerate(STEPS[:-1]))

        @pl.when(mode != 1)
        def _():
            load_rhs(r, 0)

        @pl.when(mode != 0)
        def _():
            load_rhs(r, 1)

        @pl.when(mode == 2)
        def _():
            add(r, WIDE, pl.ds(0, 2 * TOK))

        @pl.when(mode != 2)
        def _():
            add(r, BLOCK, pl.ds(pl.multiple_of(mode * TOK, TOK), TOK))

        return 0

    lax.fori_loop(0, len(STEPS) - 1, step, 0)
    todo, r, mode = STEPS[-1]
    run(todo)
    at = (own, other, pl.ds(0, 2 * TOK))[mode]
    if mode != 1:
        load_rhs(r, 0)
    if mode != 0:
        load_rhs(r, 1)
    for row in range(0, WIN, BLOCK):
        total = acc[pl.ds(row * K, BLOCK * K), :] + product(r, row, BLOCK, at)
        out[pl.ds(row, BLOCK)] = total[:, 0:WIN].reshape(BLOCK, K, WIN).astype(BF16)

    for i in range(5):
        act_whole(i).wait_send()
    for i in range(4):
        act_half(i).wait_send()
    for r in range(GROUPS):
        act_sibling(r).wait_send()
        to_sibling(r).wait_send()
        if r > 0:
            direct(r).wait_send()
        if r > 0 and r not in WHOLE:
            for hop in range(2):
                for way in range(2):
                    along_z(r, hop, way).wait_send()
        if r in SPLIT:
            to_x_lo(r).wait_send()


def local(act, grad_out, q_cols, example_order, segment):
    dma = pltpu.SemaphoreType.DMA
    return pl.pallas_call(
        kernel,
        out_shape=jax.ShapeDtypeStruct((WIN, K, WIN), BF16),
        in_specs=[pl.BlockSpec(memory_space=pltpu.HBM)] * 5,
        out_specs=pl.BlockSpec(memory_space=pltpu.VMEM),
        scratch_shapes=[
            pltpu.VMEM((GROUPS, MSG, 2 * TOK), BF16),
            pltpu.VMEM((GROUPS, TOK, SLAB), BF16),
            pltpu.VMEM((GROUPS, TOK, HALF), BF16),
            pltpu.VMEM((2 * TOK, HALF), BF16),
            pltpu.VMEM((WIN * K, HALF), F32),
            pltpu.VMEM((K, 128), F32),
            pltpu.VMEM((1, 128), jnp.int32),
            pltpu.VMEM((1, TOK), jnp.int32),
            dma((5,)),
            dma((9,)), dma((9,)), dma((GROUPS,)), dma((GROUPS,)),
            dma((GROUPS,)), dma((GROUPS,)), dma((GROUPS, 4)), dma((GROUPS, 4)),
            dma((GROUPS,)), dma((GROUPS,)), dma((GROUPS,)), dma((GROUPS,)),
        ],
        compiler_params=pltpu.CompilerParams(
            collective_id=1, has_side_effects=True, vmem_limit_bytes=48 * 1024 * 1024
        ),
    )(act.T, grad_out, q_cols.T, example_order[None, :], segment[None, :])


def solution(mesh):
    in_specs = (P("ex", "tp"), P("ex", None), P(), P(), P("ex"))
    out_specs = P("tp", None, "ex")
    return jax.shard_map(local, mesh=mesh, in_specs=in_specs, out_specs=out_specs, check_vma=False)
```

time: 143 us -> 55.2 us (0.39)
  blocking collectives: 64.6 us -> 0 us
  Pallas kernels: 0 us -> 50.2 us
  matrix products: 22 us -> 0 us
  between operations: 13.4 us -> 0.01 us
  other arithmetic: 13 us -> 0 us
  waiting for transfers between devices: 9 us -> 0 us
  starting transfers between devices: 8.48 us -> 0 us
  local copies, waits for them, and re-layouts: 12.1 us -> 4.8 us
    all_gather x1 -> x0, blocking collectives: 64.6 us -> none  [local(): lax.all_gather(segment, 'ex', axis=0, tiled=True)]
    pallas_call x0 -> x1, Pallas kernels: none -> 50.2 us  [local(): pl.pallas_call(kernel, out_shape=jax.ShapeDtypeStruct((WIN, K, WIN), BF16...]
    dot_general x3 -> x0, matrix products: 22 us -> none  [the longest x1 19.9 us: local(): lax.dot_general(all_act, scaled, (((0,), (0,)), ((), ())), preferred_elem...]
    convert_element_type x1 -> x0, other arithmetic: 10.1 us -> none  [local(): (weight[:, :, None] * grad_cols[:, None, :].astype(jnp.float32)).astype(j...]
    all_to_all x1 -> x0, starting transfers between devices: 8.45 us -> none  [local(): lax.all_to_all(grad_out, 'ex', split_axis=1, concat_axis=0, tiled=True)]
    all_gather x1 -> x0, waiting for transfers between devices: 8.32 us -> none  [local(): lax.all_gather(act, 'ex', axis=0, tiled=True)]
    convert_element_type x2 -> x0, local copies, waits for them, and re-layouts: 6.18 us -> none  [the longest x1 5.31 us: local(): return total.reshape(width_in, columns_k, width_out).astype(jnp.bfloat16)]
    unnamed x1 -> x0, other arithmetic: 2.95 us -> none
  transfers between devices with their start and end apart: 2 -> 0, of which waited for: 1 -> 0; matrix products, arithmetic and copies ran while one was open for 11% -> 0% of each run, Pallas kernels for 0% -> 0%
where the time goes in v2:
time: 55.2 us; the launch traced here: 55 us
  Pallas kernels  50.2 us (91%)
  local copies, waits for them, and re-layouts  4.8 us (9%)
    pallas_call x1, Pallas kernels, local(): pl.pallas_call(kernel, out_shape=jax.ShapeDtypeStruct((WIN, K, WIN), BF16...  50.2 us
    unnamed x9, local copies, waits for them, and re-layouts  4.8 us

profile of v2, /device:TPU:1, one launch (start us, length us, event | category | flops | bytes accessed | tf_op | source)
XLA Modules:
  0.0 55.0 jit_solution(14101779209285054282)
XLA Ops:
  0.0 0.0 copy-start
  0.0 0.9 %copy-done = bf16[256,448]{0,1:T(8,128)(2,1)S(1)} copy-done((bf16[256,448]{0,1:T(8,128)(2,1)S(1)}, bf16[256,448]{0,1:T(8,128)(2,1)}, u32[]{:S(2)}) %copy-start) | copy-done | bytes 229400
  0.9 0.0 copy-start.1
  0.9 0.7 %copy-done.1 = f32[128,8]{0,1:T(8,128)S(1)} copy-done((f32[128,8]{0,1:T(8,128)S(1)}, f32[128,8]{0,1:T(8,128)}, u32[]{:S(2)}) %copy-start.1) | copy-done | bytes 4120
  1.6 0.0 copy-start.2
  1.6 0.7 %copy-done.2 = s32[256]{0:T(256)S(1)} copy-done((s32[256]{0:T(256)S(1)}, s32[256]{0:T(256)}, u32[]{:S(2)}) %copy-start.2) | copy-done | bytes 1048
  2.3 0.0 copy-start.3
  2.3 0.7 %copy-done.3 = s32[128]{0:T(128)S(1)} copy-done((s32[128]{0:T(128)S(1)}, s32[128]{0:T(128)}, u32[]{:S(2)}) %copy-start.3) | copy-done | bytes 536
  3.0 50.2 %shard_map.55 = bf16[448,8,448]{2,1,0:T(8,128)(2,1)S(1)} custom-call(bf16[448,256]{1,0:T(8,128)(2,1)S(1)} %bitcast.4, bf16[256,7168]{1,0:T(8,128)(2,1)} %grad.1, f32[8,128]{1,0:T(8,128)S(1)} %bitcast.5, s32[1,128]{1,0:T(1,128)S(1)} %bitcast.7, s32[1,256]{1,0:T(1,128)S(1)} %bitcast.6), custom_call_target="tpu_custom_call" | custom-call | tf_op jit(solution)/shard_map/pallas_call | solution.py:393
  53.1 1.8 %copy.7 = bf16[448,8,448]{2,1,0:T(8,128)(2,1)} copy(bf16[448,8,448]{2,1,0:T(8,128)(2,1)S(1)} %shard_map.55) | data formatting | bytes 6422528
Async XLA Ops:
  0.0 0.9 %copy-start = (bf16[256,448]{0,1:T(8,128)(2,1)S(1)}, bf16[256,448]{0,1:T(8,128)(2,1)}, u32[]{:S(2)}) copy-start(bf16[256,448]{0,1:T(8,128)(2,1)} %param.5) | copy-start | bytes 688132
  0.9 0.7 %copy-start.1 = (f32[128,8]{0,1:T(8,128)S(1)}, f32[128,8]{0,1:T(8,128)}, u32[]{:S(2)}) copy-start(f32[128,8]{0,1:T(8,128)} %param.7) | copy-start | bytes 12292
  1.6 0.7 %copy-start.2 = (s32[256]{0:T(256)S(1)}, s32[256]{0:T(256)}, u32[]{:S(2)}) copy-start(s32[256]{0:T(256)} %param.9) | copy-start | bytes 3076
  2.3 0.7 %copy-start.3 = (s32[128]{0:T(128)S(1)}, s32[128]{0:T(128)}, u32[]{:S(2)}) copy-start(s32[128]{0:T(128)} %param.8) | copy-start | bytes 1540

commit v3 on v2

--- a/solution.py
+++ b/solution.py
@@ -26,12 +26,15 @@
     (GO, 'columns', 0),
     (GO, 'direct', 4),
     (GO, 'direct', 2),
-    (GO, 'act', 0),
+    (GO, 'act', 0, 0),
+    (GO, 'act', 0, 1),
     (GO, 'direct', 7),
     (GO, 'direct', 5),
-    (GO, 'act', 1),
+    (GO, 'act', 1, 0),
+    (GO, 'act', 1, 1),
     (GO, 'direct', 1),
-    (GO, 'act', 2),
+    (GO, 'act', 2, 0),
+    (GO, 'act', 2, 1),
 )
 STEPS = (
     ((), 0, 0),
@@ -62,11 +65,14 @@
         (GET, 'z_second', 2, 0),
         (GET, 'z_second', 2, 1),
         (GO, 'x_lo', 2),
-        (GET, 'act', 0),
+        (GET, 'act', 0, 0),
+        (GET, 'act', 0, 1),
         (GO, 'act_core', 3),
-        (GO, 'act', 4),
+        (GO, 'act', 4, 0),
+        (GO, 'act', 4, 1),
         (GET, 'direct', 7),
-        (GO, 'act', 3),
+        (GO, 'act', 3, 0),
+        (GO, 'act', 3, 1),
         (GO, 'z_first', 7, 0),
         (GO, 'z_first', 7, 1),
         (GET, 'act_core', 3),
@@ -77,9 +83,11 @@
         (GET, 'z_second', 4, 1),
         (GET, 'z_second', 4, 0),
         (GO, 'x_lo', 4),
-        (GET, 'act', 1),
+        (GET, 'act', 1, 0),
+        (GET, 'act', 1, 1),
         (GO, 'act_core', 2),
-        (GET, 'act', 2),
+        (GET, 'act', 2, 0),
+        (GET, 'act', 2, 1),
         (GO, 'act_core', 1),
         (GO, 'act_half', 0),
         (GO, 'act_half', 1),
@@ -121,9 +129,11 @@
         (GET, 'z_first', 6, 1),
         (GO, 'z_second', 6, 1),
         (GO, 'z_second', 6, 0),
-        (GET, 'act', 4),
+        (GET, 'act', 4, 0),
+        (GET, 'act', 4, 1),
         (GO, 'act_core', 4),
-        (GET, 'act', 3),
+        (GET, 'act', 3, 0),
+        (GET, 'act', 3, 1),
         (GO, 'act_core', 5),
         (GO, 'act_half', 3),
         (GO, 'act_half', 2),
@@ -169,9 +179,30 @@
     ), 7, 2),
 )
 
+def product(a, rhs, row, size, at):
+    w = a[WIN:WIN + 32, at].astype(F32)
+    w = w[0:8] + w[8:16] + w[16:24]
+    left = a[pl.ds(row, size), at].astype(F32)
+    left = (left[:, None, :] * w[None, :, :]).astype(BF16).reshape(size * K, at.size)
+    return jnp.dot(left, rhs[at, :], preferred_element_type=F32)
+
+
+def finish(acc, a_last, rhs, out, stage, sem):
+    at = (pl.ds(0, TOK), pl.ds(TOK, TOK), pl.ds(0, 2 * TOK))[STEPS[-1][2]]
+    copies = []
+    for i, row in enumerate(range(0, WIN, BLOCK)):
+        total = acc[pl.ds(row * K, BLOCK * K), :] + product(a_last, rhs, row, BLOCK, at)
+        stage[pl.ds(row, BLOCK)] = total[:, 0:WIN].reshape(BLOCK, K, WIN).astype(BF16)
+        rows = pl.ds(row, BLOCK)
+        copies.append(pltpu.make_async_copy(stage.at[rows], out.at[rows], sem.at[i]))
+        copies[-1].start()
+    for copy in copies:
+        copy.wait()
+
+
 def kernel(
-    act, grad, q_cols, order, segment, out,
-    a_buf, g_buf, h_buf, rhs, acc, q_buf, order_buf, segment_buf, local_sem,
+    act, grad, q_cols, order, segment, acc, a_last, rhs,
+    a_buf, g_buf, h_buf, q_buf, order_buf, segment_buf, local_sem,
     a_send, a_recv, as_send, as_recv, d_send, d_recv, z_send, z_recv, x_send, x_recv, h_send, h_recv,
 ):
     e, t = lax.axis_index("ex"), lax.axis_index("tp")
@@ -210,6 +241,89 @@
     ]
     for load in loads:
         load.start()
+    def quarter(r, q, side, half=None):
+        if r in WHOLE:
+            return pl.ds(0, TOK)
+        rows = TOK // 8 if r in SPLIT else TOK // 4
+        at = q * rows + (side * (TOK // 2) if r in SPLIT else 0)
+        if half is not None:
+            rows = rows // 2
+            at = at + half * rows
+        return pl.ds(pl.multiple_of(at, rows), rows)
+
+    def direct(r):
+        dx, dy = SOURCES[r]
+        to_x, to_y = (xh + dx) % NX, (y - dy + NY) % NY
+        lanes = pl.ds(pl.multiple_of(SLAB * (4 * to_x + to_y), 128), SLAB)
+        rows = quarter(r, share, (xl + dx) % 2)
+        return remote(
+            grad.at[rows, lanes], g_buf.at[r, rows, :], d_send.at[r], d_recv.at[r], dev(dx, -dy, dl=dx)
+        )
+
+    def direct_in(r):
+        part = g_buf.at[r, quarter(r, share, xl), :]
+        return remote(part, part, d_send.at[r], d_recv.at[r], dev(dc=1))
+
+    def along_z(r, hop, way):
+        if hop == 0:
+            at = quarter(r, share, xl)
+        else:
+            at = quarter(r, (share + (3 if way == 0 else 1)) % 4, xl, way)
+        part = g_buf.at[r, at, :]
+        i = hop * 2 + way
+        return remote(part, part, z_send.at[r, i], z_recv.at[r, i], dev(dz=1 if way == 0 else -1))
+
+    def to_x_lo(r):
+        half = TOK // 2
+        part = g_buf.at[r, pl.ds(pl.multiple_of(xl * half, half), half), :]
+        return remote(part, part, x_send.at[r], x_recv.at[r], dev(dl=1))
+
+    def to_sibling(r):
+        lanes = pl.ds(pl.multiple_of(384 * (1 - c), 128), HALF)
+        return remote(g_buf.at[r, :, lanes], h_buf.at[r], h_send.at[r], h_recv.at[r], dev(dc=1))
+
+    def act_part(src, dst, half, to, i):
+        at = pl.ds(half * (MSG // 2), MSG // 2)
+        return remote(a_buf.at[src, at, own], a_buf.at[dst, at, own], a_send.at[i], a_recv.at[i], to)
+
+    def act_whole(i, half):
+        src, dst, to = [
+            (0, 3, dev(dx=1)),
+            (0, 2, dev(dy=1)), (0, 1, dev(dy=-1)),
+            (3, 5, dev(dy=1)), (3, 4, dev(dy=-1)),
+        ][i]
+        return act_part(src, dst, half, to, 2 * i + half)
+
+    def act_half(i):
+        src, dst, to = [(2, 6, dev(dy=1)), (1, 6, dev(dy=-1)), (5, 7, dev(dy=1)), (4, 7, dev(dy=-1))][i]
+        return act_part(src, dst, i % 2, to, 10 + i)
+
+    def act_over_x(half):
+        return act_part(6, 7, half, dev(dx=1), 14 + half)
+
+    def act_sibling(r):
+        return remote(
+            a_buf.at[r, :, own], a_buf.at[r, :, other], as_send.at[r], as_recv.at[r], dev(dc=1)
+        )
+
+    transfers = {
+        "direct": direct, "x_lo": to_x_lo, "columns": to_sibling,
+        "z_first": lambda r, way: along_z(r, 0, way), "z_second": lambda r, way: along_z(r, 1, way),
+        "act": act_whole, "act_half": act_half,
+        "act_over_x": act_over_x, "act_core": act_sibling,
+    }
+
+    def run(todo):
+        for go, name, *which in todo:
+            if go:
+                transfers[name](*which).start()
+            else:
+                (direct_in if name == "direct" else transfers[name])(*which).wait_recv()
+
+    pl.semaphore_wait(barrier, len(peers))
+    early = [item for item in FIRST if item[1] == "direct"]
+    run(early)
+
     rhs[...] = jnp.zeros_like(rhs)
     acc[...] = jnp.zeros_like(acc)
     for load in loads[:3]:
@@ -229,86 +343,7 @@
     a_buf[0, pl.ds(WIN, MSG - WIN), own] = weights.astype(BF16)
     loads[3].wait()
 
-    pl.semaphore_wait(barrier, len(peers))
-
-    def quarter(r, q, side, half=None):
-        if r in WHOLE:
-            return pl.ds(0, TOK)
-        rows = TOK // 8 if r in SPLIT else TOK // 4
-        at = q * rows + (side * (TOK // 2) if r in SPLIT else 0)
-        if half is not None:
-            rows = rows // 2
-            at = at + half * rows
-        return pl.ds(pl.multiple_of(at, rows), rows)
-
-    def direct(r):
-        dx, dy = SOURCES[r]
-        to_x, to_y = (xh + dx) % NX, (y - dy + NY) % NY
-        lanes = pl.ds(pl.multiple_of(SLAB * (4 * to_x + to_y), 128), SLAB)
-        rows = quarter(r, share, (xl + dx) % 2)
-        return remote(
-            grad.at[rows, lanes], g_buf.at[r, rows, :], d_send.at[r], d_recv.at[r], dev(dx, -dy, dl=dx)
-        )
-
-    def direct_in(r):
-        part = g_buf.at[r, quarter(r, share, xl), :]
-        return remote(part, part, d_send.at[r], d_recv.at[r], dev(dc=1))
-
-    def along_z(r, hop, way):
-        if hop == 0:
-            at = quarter(r, share, xl)
-        else:
-            at = quarter(r, (share + (3 if way == 0 else 1)) % 4, xl, way)
-        part = g_buf.at[r, at, :]
-        i = hop * 2 + way
-        return remote(part, part, z_send.at[r, i], z_recv.at[r, i], dev(dz=1 if way == 0 else -1))
-
-    def to_x_lo(r):
-        half = TOK // 2
-        part = g_buf.at[r, pl.ds(pl.multiple_of(xl * half, half), half), :]
-        return remote(part, part, x_send.at[r], x_recv.at[r], dev(dl=1))
-
-    def to_sibling(r):
-        lanes = pl.ds(pl.multiple_of(384 * (1 - c), 128), HALF)
-        return remote(g_buf.at[r, :, lanes], h_buf.at[r], h_send.at[r], h_recv.at[r], dev(dc=1))
-
-    def act_whole(i):
-        src, dst, to = [
-            (0, 3, dev(dx=1)),
-            (0, 2, dev(dy=1)), (0, 1, dev(dy=-1)),
-            (3, 5, dev(dy=1)), (3, 4, dev(dy=-1)),
-        ][i]
-        return remote(a_buf.at[src, :, own], a_buf.at[dst, :, own], a_send.at[i], a_recv.at[i], to)
-
-    def act_half(i):
-        src, dst, to, at = [
-            (2, 6, dev(dy=1), 0), (1, 6, dev(dy=-1), MSG // 2),
-            (5, 7, dev(dy=1), 0), (4, 7, dev(dy=-1), MSG // 2),
-        ][i]
-        at = pl.ds(at, MSG // 2)
-        return remote(
-            a_buf.at[src, at, own], a_buf.at[dst, at, own], a_send.at[5 + i], a_recv.at[5 + i], to
-        )
-
-    def act_sibling(r):
-        return remote(
-            a_buf.at[r, :, own], a_buf.at[r, :, other], as_send.at[r], as_recv.at[r], dev(dc=1)
-        )
-
-    transfers = {
-        "direct": direct, "x_lo": to_x_lo, "columns": to_sibling,
-        "z_first": lambda r, way: along_z(r, 0, way), "z_second": lambda r, way: along_z(r, 1, way),
-        "act": act_whole, "act_half": act_half, "act_core": act_sibling,
-    }
-
-    def run(todo):
-        for go, name, *which in todo:
-            if go:
-                transfers[name](*which).start()
-            else:
-                (direct_in if name == "direct" else transfers[name])(*which).wait_recv()
-
-    run([item for item in FIRST if item[1:] != ("columns", 0)])
+    run([item for item in FIRST if item not in early and item[1] != "columns"])
     loads[4].wait()
     to_sibling(0).start()
 
@@ -323,16 +358,9 @@
         def _():
             rhs[at, 0:WIN] = g_buf[r, :, SLAB - WIN:SLAB] if half == 0 else h_buf[r, :, HALF - WIN:HALF]
 
-    def product(r, row, size, at):
-        w = a_buf[r, WIN:WIN + 32, at].astype(F32)
-        w = w[0:8] + w[8:16] + w[16:24]
-        part = a_buf[r, pl.ds(row, size), at].astype(F32)
-        left = (part[:, None, :] * w[None, :, :]).astype(BF16).reshape(size * K, at.size)
-        return jnp.dot(left, rhs[at, :], preferred_element_type=F32)
-
     def add(r, size, at):
         for row in range(0, WIN, size):
-            acc[pl.ds(row * K, size * K), :] += product(r, row, size, at)
+            acc[pl.ds(row * K, size * K), :] += product(a_buf.at[r], rhs, row, size, at)
 
     def step(n, _):
         for i, (todo, _, _) in enumerate(STEPS[:-1]):
@@ -362,57 +390,58 @@
     lax.fori_loop(0, len(STEPS) - 1, step, 0)
     todo, r, mode = STEPS[-1]
     run(todo)
-    at = (own, other, pl.ds(0, 2 * TOK))[mode]
     if mode != 1:
         load_rhs(r, 0)
     if mode != 0:
         load_rhs(r, 1)
-    for row in range(0, WIN, BLOCK):
-        total = acc[pl.ds(row * K, BLOCK * K), :] + product(r, row, BLOCK, at)
-        out[pl.ds(row, BLOCK)] = total[:, 0:WIN].reshape(BLOCK, K, WIN).astype(BF16)
-
-    for i in range(5):
-        act_whole(i).wait_send()
-    for i in range(4):
-        act_half(i).wait_send()
-    for r in range(GROUPS):
-        act_sibling(r).wait_send()
-        to_sibling(r).wait_send()
-        if r > 0:
-            direct(r).wait_send()
-        if r > 0 and r not in WHOLE:
-            for hop in range(2):
-                for way in range(2):
-                    along_z(r, hop, way).wait_send()
-        if r in SPLIT:
-            to_x_lo(r).wait_send()
+    a_last[...] = a_buf[r]
+
+    for todo in [FIRST] + [step[0] for step in STEPS]:
+        for go, name, *which in todo:
+            if go:
+                transfers[name](*which).wait_send()
 
 
 def local(act, grad_out, q_cols, example_order, segment):
     dma = pltpu.SemaphoreType.DMA
-    return pl.pallas_call(
+    hbm = [
+        pltpu.with_memory_space_constraint(v, pltpu.HBM)
+        for v in (act.T, grad_out, q_cols.T, example_order[None, :], segment[None, :])
+    ]
+    vmem = pl.BlockSpec(memory_space=pltpu.VMEM)
+    parts = pl.pallas_call(
         kernel,
-        out_shape=jax.ShapeDtypeStruct((WIN, K, WIN), BF16),
+        out_shape=[
+            jax.ShapeDtypeStruct((WIN * K, HALF), F32),
+            jax.ShapeDtypeStruct((MSG, 2 * TOK), BF16),
+            jax.ShapeDtypeStruct((2 * TOK, HALF), BF16),
+        ],
         in_specs=[pl.BlockSpec(memory_space=pltpu.HBM)] * 5,
-        out_specs=pl.BlockSpec(memory_space=pltpu.VMEM),
+        out_specs=[vmem] * 3,
         scratch_shapes=[
             pltpu.VMEM((GROUPS, MSG, 2 * TOK), BF16),
             pltpu.VMEM((GROUPS, TOK, SLAB), BF16),
             pltpu.VMEM((GROUPS, TOK, HALF), BF16),
-            pltpu.VMEM((2 * TOK, HALF), BF16),
-            pltpu.VMEM((WIN * K, HALF), F32),
             pltpu.VMEM((K, 128), F32),
             pltpu.VMEM((1, 128), jnp.int32),
             pltpu.VMEM((1, TOK), jnp.int32),
             dma((5,)),
-            dma((9,)), dma((9,)), dma((GROUPS,)), dma((GROUPS,)),
+            dma((16,)), dma((16,)), dma((GROUPS,)), dma((GROUPS,)),
             dma((GROUPS,)), dma((GROUPS,)), dma((GROUPS, 4)), dma((GROUPS, 4)),
             dma((GROUPS,)), dma((GROUPS,)), dma((GROUPS,)), dma((GROUPS,)),
         ],
         compiler_params=pltpu.CompilerParams(
-            collective_id=1, has_side_effects=True, vmem_limit_bytes=48 * 1024 * 1024
+            collective_id=1, has_side_effects=True, vmem_limit_bytes=24 * 1024 * 1024
         ),
-    )(act.T, grad_out, q_cols.T, example_order[None, :], segment[None, :])
+    )(*hbm)
+    return pl.pallas_call(
+        finish,
+        out_shape=jax.ShapeDtypeStruct((WIN, K, WIN), BF16),
+        in_specs=[vmem] * 3,
+        out_specs=pl.BlockSpec(memory_space=pltpu.HBM),
+        scratch_shapes=[pltpu.VMEM((WIN, K, WIN), BF16), dma((WIN // BLOCK,))],
+        compiler_params=pltpu.CompilerParams(vmem_limit_bytes=16 * 1024 * 1024),
+    )(*[pltpu.with_memory_space_constraint(v, pltpu.VMEM) for v in parts])
 
 
 def solution(mesh):

time: 55.2 us -> 50.7 us (0.918)
  local copies, waits for them, and re-layouts: 4.8 us -> 0 us
    unnamed x9 -> x0, local copies, waits for them, and re-layouts: 4.8 us -> none
    pallas_call x1 -> x2, Pallas kernels: 50.2 us -> 50.6 us  [the longest x1 47.6 us: local(): pl.pallas_call(kernel, out_shape=[jax.ShapeDtypeStruct((WIN * K, HALF), F...]
where the time goes in v3:
time: 50.7 us; the launch traced here: 50.6 us
  Pallas kernels  50.6 us (100%)
    pallas_call x1, Pallas kernels, local(): pl.pallas_call(kernel, out_shape=[jax.ShapeDtypeStruct((WIN * K, HALF), F...  47.6 us
    pallas_call x1, Pallas kernels, local(): pl.pallas_call(finish, out_shape=jax.ShapeDtypeStruct((WIN, K, WIN), BF16...  3.03 us

profile of v3, /device:TPU:1, one launch (start us, length us, event | category | flops | bytes accessed | tf_op | source)
XLA Modules:
  0.0 50.6 jit_solution(1102293064191960233)
XLA Ops:
  0.0 47.6 %shard_map.55 = (f32[3584,512]{1,0:T(8,128)S(1)}, bf16[480,512]{1,0:T(8,128)(2,1)S(1)}, bf16[512,512]{1,0:T(8,128)(2,1)S(1)}) custom-call(bf16[448,256]{1,0:T(8,128)(2,1)} %bitcast.4, bf16[256,7168]{1,0:T(8,128)(2,1)} %grad.1, f32[8,128]{1,0:T(8,128)} %bitcast.5, s32[1,128]{1,0:T(1,128)} %bitcast.7, s32[1,256]{1,0:T(1,128)} %bitcast.6), custom_call_target="tpu_custom_call" | custom-call | tf_op jit(solution)/shard_map/pallas_call | solution.py:412
  47.6 3.0 %shard_map.56 = bf16[448,8,448]{2,1,0:T(8,128)(2,1)} custom-call(f32[3584,512]{1,0:T(8,128)S(1)} %get-tuple-element.8.acc, bf16[480,512]{1,0:T(8,128)(2,1)S(1)} %get-tuple-element.9.a_last, bf16[512,512]{1,0:T(8,128)(2,1)S(1)} %get-tuple-element.10.rhs), custom_call_target="tpu_custom_call" | custom-call | tf_op jit(solution)/shard_map/pallas_call | solution.py:437

commit v4 on v3

--- a/solution.py
+++ b/solution.py
@@ -14,6 +14,7 @@
 HALF = 512
 MSG = 480
 K = 8
+FINE = 64
 BLOCK = 112
 WIDE = 224
 SOURCES = ((0, 0), (0, 1), (0, 3), (1, 0), (1, 1), (1, 3), (0, 2), (1, 2))
@@ -190,10 +191,10 @@
 def finish(acc, a_last, rhs, out, stage, sem):
     at = (pl.ds(0, TOK), pl.ds(TOK, TOK), pl.ds(0, 2 * TOK))[STEPS[-1][2]]
     copies = []
-    for i, row in enumerate(range(0, WIN, BLOCK)):
-        total = acc[pl.ds(row * K, BLOCK * K), :] + product(a_last, rhs, row, BLOCK, at)
-        stage[pl.ds(row, BLOCK)] = total[:, 0:WIN].reshape(BLOCK, K, WIN).astype(BF16)
-        rows = pl.ds(row, BLOCK)
+    for i, row in enumerate(range(0, WIN, FINE)):
+        total = acc[pl.ds(row * K, FINE * K), :] + product(a_last, rhs, row, FINE, at)
+        stage[pl.ds(row, FINE)] = total[:, 0:WIN].reshape(FINE, K, WIN).astype(BF16)
+        rows = pl.ds(row, FINE)
         copies.append(pltpu.make_async_copy(stage.at[rows], out.at[rows], sem.at[i]))
         copies[-1].start()
     for copy in copies:
@@ -439,7 +440,7 @@
         out_shape=jax.ShapeDtypeStruct((WIN, K, WIN), BF16),
         in_specs=[vmem] * 3,
         out_specs=pl.BlockSpec(memory_space=pltpu.HBM),
-        scratch_shapes=[pltpu.VMEM((WIN, K, WIN), BF16), dma((WIN // BLOCK,))],
+        scratch_shapes=[pltpu.VMEM((WIN, K, WIN), BF16), dma((WIN // FINE,))],
         compiler_params=pltpu.CompilerParams(vmem_limit_bytes=16 * 1024 * 1024),
     )(*[pltpu.with_memory_space_constraint(v, pltpu.VMEM) for v in parts])
 

time: 50.7 us -> 50.6 us (level)
  no operation moved by 1% of the time
where the time goes in v4:
time: 50.6 us; the launch traced here: 50.5 us
  Pallas kernels  50.5 us (100%)
    pallas_call x1, Pallas kernels, local(): pl.pallas_call(kernel, out_shape=[jax.ShapeDtypeStruct((WIN * K, HALF), F...  47.6 us
    pallas_call x1, Pallas kernels, local(): pl.pallas_call(finish, out_shape=jax.ShapeDtypeStruct((WIN, K, WIN), BF16...  2.93 us

profile of v4, /device:TPU:1, one launch (start us, length us, event | category | flops | bytes accessed | tf_op | source)
XLA Modules:
  0.0 50.5 jit_solution(17238373634647234782)
XLA Ops:
  0.0 47.6 %shard_map.55 = (f32[3584,512]{1,0:T(8,128)S(1)}, bf16[480,512]{1,0:T(8,128)(2,1)S(1)}, bf16[512,512]{1,0:T(8,128)(2,1)S(1)}) custom-call(bf16[448,256]{1,0:T(8,128)(2,1)} %bitcast.4, bf16[256,7168]{1,0:T(8,128)(2,1)} %grad.1, f32[8,128]{1,0:T(8,128)} %bitcast.5, s32[1,128]{1,0:T(1,128)} %bitcast.7, s32[1,256]{1,0:T(1,128)} %bitcast.6), custom_call_target="tpu_custom_call" | custom-call | tf_op jit(solution)/shard_map/pallas_call | solution.py:413
  47.6 2.9 %shard_map.56 = bf16[448,8,448]{2,1,0:T(8,128)(2,1)} custom-call(f32[3584,512]{1,0:T(8,128)S(1)} %get-tuple-element.8.acc, bf16[480,512]{1,0:T(8,128)(2,1)S(1)} %get-tuple-element.9.a_last, bf16[512,512]{1,0:T(8,128)(2,1)S(1)} %get-tuple-element.10.rhs), custom_call_target="tpu_custom_call" | custom-call | tf_op jit(solution)/shard_map/pallas_call | solution.py:438

commit v5 on v4

--- a/solution.py
+++ b/solution.py
@@ -15,8 +15,8 @@
 MSG = 480
 K = 8
 FINE = 64
-BLOCK = 112
-WIDE = 224
+BLOCK = 224
+WIDE = 448
 SOURCES = ((0, 0), (0, 1), (0, 3), (1, 0), (1, 1), (1, 3), (0, 2), (1, 2))
 GROUPS = len(SOURCES)
 WHOLE = (3,)

time: 50.6 us -> 50.6 us (level)
  no operation moved by 1% of the time
where the time goes in v5:
time: 50.6 us; the launch traced here: 50.5 us
  Pallas kernels  50.5 us (100%)
    pallas_call x1, Pallas kernels, local(): pl.pallas_call(kernel, out_shape=[jax.ShapeDtypeStruct((WIN * K, HALF), F...  47.6 us
    pallas_call x1, Pallas kernels, local(): pl.pallas_call(finish, out_shape=jax.ShapeDtypeStruct((WIN, K, WIN), BF16...  2.93 us

profile of v5, /device:TPU:1, one launch (start us, length us, event | category | flops | bytes accessed | tf_op | source)
XLA Modules:
  0.0 50.5 jit_solution(6680303231131715953)
XLA Ops:
  0.0 47.6 %shard_map.55 = (f32[3584,512]{1,0:T(8,128)S(1)}, bf16[480,512]{1,0:T(8,128)(2,1)S(1)}, bf16[512,512]{1,0:T(8,128)(2,1)S(1)}) custom-call(bf16[448,256]{1,0:T(8,128)(2,1)} %bitcast.4, bf16[256,7168]{1,0:T(8,128)(2,1)} %grad.1, f32[8,128]{1,0:T(8,128)} %bitcast.5, s32[1,128]{1,0:T(1,128)} %bitcast.7, s32[1,256]{1,0:T(1,128)} %bitcast.6), custom_call_target="tpu_custom_call" | custom-call | tf_op jit(solution)/shard_map/pallas_call | solution.py:413
  47.6 2.9 %shard_map.56 = bf16[448,8,448]{2,1,0:T(8,128)(2,1)} custom-call(f32[3584,512]{1,0:T(8,128)S(1)} %get-tuple-element.8.acc, bf16[480,512]{1,0:T(8,128)(2,1)S(1)} %get-tuple-element.9.a_last, bf16[512,512]{1,0:T(8,128)(2,1)S(1)} %get-tuple-element.10.rhs), custom_call_target="tpu_custom_call" | custom-call | tf_op jit(solution)/shard_map/pallas_call | solution.py:438
